TPU v7x, 32 devices: a whole 2x2x4 slice. The times are simulated.
32 devices in a mesh: section: 2 (over x), fsdp: 16 (over z, y, core).
Axes of the slice: x: 2, y: 2, z: 4, core: 2. Of those that a mesh axis runs over, the one named last changes fastest.
Arguments:
- activations: bfloat16 [2560, 6144], P('fsdp'), may hold values from -36 to 36
- keep: int32 [2560], P('fsdp'), may hold values from 0 to 1, as said below
- gains: bfloat16 [2, 6144], P('section'), may hold values from 0.099609375 to 1.8984375
- up_rows: int32 [2, 192, 2], P('section'), may hold values from 0 to 95
- up_blocks: bfloat16 [2, 384, 4096], P('section', 'fsdp'), may hold values from -0.5 to 0.5
- down_rows: int32 [2, 96, 2], P('section'), may hold values from 0 to 191
- down_blocks: bfloat16 [2, 192, 4096], P('section', 'fsdp'), may hold values from -0.5 to 0.5
Outputs:
- section_out: bfloat16 [2, 2560, 6144], P('section', 'fsdp')
Inputs may be any that keep to these rules, and one draw needn't show every extreme that they name: `keep`: each aligned block of 160 tokens (the tokens of one index of fsdp) holds exactly 128 ones.
All inputs are finite; a program needn't handle non-finite values.
Results may differ from a plain program's by a relative error of at most 0.012.
Values may be sent and summed in bfloat16 or wider, within the bound.
A program may use at most 128 MiB of HBM per device.

v0:
```python
import jax
import jax.numpy as jnp
from jax import lax
from jax.sharding import PartitionSpec as P

BLK = 64
UP_DEPTH = 2
DOWN_DEPTH = 2
KEEP_DEV = 128


def from_behind(value, axis, steps):
    count = lax.axis_size(axis)
    initial, last = (max(0, -steps), min(count, count - steps))
    return lax.ppermute(value, axis, [(source, source + steps) for source in range(initial, last)])


def make_layer(gain, up_index, up_values, down_index, down_values):
    width = gain.shape[0]
    hidden_width = up_values.shape[0] // UP_DEPTH * BLK
    blocks_in = width // BLK
    blocks_hid = hidden_width // BLK
    weights_up = up_values.reshape(blocks_hid, UP_DEPTH * BLK, BLK)
    weights_down = down_values.reshape(blocks_in, DOWN_DEPTH * BLK, BLK)
    gain_wide = gain.astype(jnp.float32)

    def layer(block):
        count = block.shape[0]
        wide = block.astype(jnp.float32)
        meansq = jnp.mean(wide * wide, axis=-1, keepdims=True)
        normed = (wide * lax.rsqrt(meansq + 1e-05) * gain_wide).astype(jnp.bfloat16)
        picked = normed.reshape(count, blocks_in, BLK)[:, up_index, :]
        picked = picked.reshape(count, blocks_hid, UP_DEPTH * BLK)
        up_sums = jnp.einsum("ncr,crj->ncj", picked, weights_up, preferred_element_type=jnp.float32)
        hidden = jax.nn.gelu(up_sums, approximate=True).astype(jnp.bfloat16)
        second = hidden[:, down_index, :].reshape(count, blocks_in, DOWN_DEPTH * BLK)
        down_sums = jnp.einsum(
            "ncr,crj->ncj", second, weights_down, preferred_element_type=jnp.float32
        )
        return (wide + down_sums.reshape(count, width)).astype(jnp.bfloat16)

    return layer


def per_device(activations, keep, gains, up_rows, up_blocks, down_rows, down_blocks):
    up_all, down_all = (
        lax.all_gather(up_blocks, "fsdp", axis=1, tiled=True),
        lax.all_gather(down_blocks, "fsdp", axis=1, tiled=True),
    )
    apply = make_layer(
        gains[0], up_rows[0].reshape(-1), up_all[0], down_rows[0].reshape(-1), down_all[0]
    )
    places = jnp.cumsum(keep) - 1
    target = jnp.where(keep == 1, places, KEEP_DEV)
    chosen = (
        jnp.zeros((KEEP_DEV + 1,), jnp.int32)
        .at[target]
        .set(jnp.arange(keep.shape[0], dtype=jnp.int32))[:KEEP_DEV]
    )
    selected = activations[chosen]
    width = selected.shape[1]
    section = lax.axis_index("section")
    sections = lax.axis_size("section")
    pieces = 8
    group_rows = selected.shape[0] // pieces
    split = selected.reshape(pieces, group_rows, width)

    def advance(turn, held, record):
        offset = turn - section
        entry = jnp.where(section == 0, split[jnp.minimum(turn, pieces - 1)], held)
        active = (offset >= 0) & (offset < pieces)
        result = lax.cond(active, apply, jnp.zeros_like, entry)
        slot = jnp.clip(offset, 0, pieces - 1)
        current = lax.dynamic_index_in_dim(record, slot, 0, keepdims=False)
        updated = jnp.where(active, result, current)
        record = lax.dynamic_update_index_in_dim(record, updated, slot, 0)
        return (result, record)

    def turn_step(turn, carry):
        held, record = carry
        result, record = advance(turn, held, record)
        held = from_behind(result, "section", 1)
        return (held, record)

    final_turn = sections + pieces - 2
    held, record = lax.fori_loop(0, final_turn, turn_step, (split[0], split))
    result, record = advance(final_turn, held, record)
    final = record.reshape(selected.shape[0], width)
    merged = activations.at[chosen].set(final)
    return merged[None]


def solution(mesh):
    return jax.shard_map(
        per_device,
        mesh=mesh,
        in_specs=(
            P("fsdp", None),
            P("fsdp"),
            P("section", None),
            P("section", None, None),
            P("section", "fsdp", None),
            P("section", None, None),
            P("section", "fsdp", None),
        ),
        out_specs=P("section", "fsdp", None),
        check_vma=False,
    )
```

profile of v0, /device:TPU:2, one launch (start us, length us, event | category | flops | bytes accessed | tf_op | source)
XLA Modules:
  0.0 380.9 jit_solution(8686544126871121145)
XLA Ops:
  19.0 37.1 %all-gather.5.cloned.1.call-done = bf16[1,192,4096]{2,0,1:T(2,128)(2,1)} async-done(((bf16[1,12,4096]{2,0,1:T(2,128)(2,1)}), bf16[1,192,4096]{2,0,1:T(2,128)(2,1)}) %all-gather.5.cloned.1.call-update) | async-done | bytes 1572880 | tf_op jit(solution)/shard_map/all_gather | solution.py:48
  56.1 12.3 %reduce.1 = bf16[192,4096]{1,0:T(8,128)(2,1)} reduce(bf16[1,192,4096]{2,0,1:T(2,128)(2,1)} %all-gather.5.cloned.1.call-done, bf16[]{:T(256)} %constant.158), dimensions={0}, to_apply=%all_gather.7.reduce_sub_computation | reduce | bytes 3145730 | tf_op jit(solution)/shard_map/all_gather | solution.py:48
  68.4 5.6 %reshape_squeeze.15 = bf16[96,128,64]{2,1,0:T(8,128)(2,1)} reshape(bf16[192,4096]{1,0:T(8,128)(2,1)} %reduce.1) | data formatting | bytes 3145728 | tf_op jit(solution)/shard_map/reshape;squeeze | solution.py:24
  74.0 4.3 %copy.42 = bf16[96,128,64]{1,2,0:T(8,128)(2,1)} copy(bf16[96,128,64]{2,1,0:T(8,128)(2,1)} %reshape_squeeze.15) | data formatting | bytes 3145728 | tf_op jit(solution)/shard_map/while | solution.py:86
  78.3 24.2 %all-gather.3.cloned.1.call-done = bf16[1,384,4096]{2,1,0:T(8,128)(2,1)} async-done(((bf16[1,24,4096]{2,1,0:T(8,128)(2,1)}), bf16[1,384,4096]{2,1,0:T(8,128)(2,1)}) %all-gather.3.cloned.1.call-update) | async-done | bytes 3145744 | tf_op jit(solution)/shard_map/all_gather | solution.py:47
  102.4 9.6 %reshape_squeeze.13 = bf16[192,128,64]{2,1,0:T(8,128)(2,1)} reshape(bf16[1,384,4096]{2,1,0:T(8,128)(2,1)} %all-gather.3.cloned.1.call-done) | data formatting | bytes 6291456 | tf_op jit(solution)/shard_map/reshape;squeeze | solution.py:23
  112.1 6.7 %copy.41 = bf16[192,128,64]{1,2,0:T(8,128)(2,1)} copy(bf16[192,128,64]{2,1,0:T(8,128)(2,1)} %reshape_squeeze.13) | data formatting | bytes 6291456 | tf_op jit(solution)/shard_map/while | solution.py:86
  118.8 209.1 %while.16 = (s32[]{:T(128)}, bf16[16,6144]{1,0:T(8,128)(2,1)S(1)}, bf16[8,16,6144]{2,1,0:T(8,128)(2,1)}, s32[]{:T(128)}, pred[]{:T(512)}, /*index=5*/bf16[8,16,6...) while((s32[]{:T(128)}, bf16[16,6144]{1,0:T(8,128)(2,1)S(1)}, ...), condition=%wide.region_7.8_spmd, body=%wide.region_3.0_spmd.sunk | while | flops 78450392 | bytes 21276344 | solution.py:86
  122.4 22.0 %collective-permute-done = bf16[16,6144]{1,0:T(8,128)(2,1)S(1)} collective-permute-done((bf16[16,6144]{1,0:T(8,128)(2,1)}, bf16[16,6144]{1,0:T(8,128)(2,1)S(1)}, u32[]{:S(2)}, u32[]{:S(2)}) %collective-permute-start) | collective-permute-done | bytes 196640 | tf_op jit(solution)/shard_map/while/body/eval_jaxpr/ppermute | solution.py:15
  144.4 18.3 %conditional.4 = (bf16[16,6144]{1,0:T(8,128)(2,1)}) conditional(s32[]{:T(128)} %convert_element_type.82, () %tuple.59, (pred[]{:T(512)}, s32[]{:T(128)}, bf16[8,16,6144]{2,1,0:T(8,128)(2,1)}, bf16[16,6144]{1,0:T(8,128)(2,1)S(1)}, f32[6144]{0:T(1024)}, /*index=5*/s32[384]{0:T(512)S(1)}, bf16[192,128,64]{1,2,0:T(8,128)(2,1)}, s32[192]{0:T(256)S(1)}, ...), branch_computations={%region_4.4_spmd, %region_5.6_spmd} | conditional | flops 78352080 | bytes 19506548 | solution.py:72
  153.5 3.9 %fusion.7 = bf16[16,192,64]{2,0,1:T(8,128)(2,1)S(1)} fusion(bf16[192,128,64]{1,2,0:T(8,128)(2,1)} %get-tuple-element.325, bf16[16,192,128]{2,1,0:T(8,128)(2,1)} %reshape.66), kind=kOutput, calls=%fused_computation.15 | convolution fusion | flops 52101120 | bytes 4325376 | tf_op jit(solution)/shard_map/while/body/eval_jaxpr/cond/branch_1_fun/ncr,crj->ncj/dot_general | solution.py:34
  166.7 4.8 %collective-permute-done = bf16[16,6144]{1,0:T(8,128)(2,1)S(1)} collective-permute-done((bf16[16,6144]{1,0:T(8,128)(2,1)}, bf16[16,6144]{1,0:T(8,128)(2,1)S(1)}, u32[]{:S(2)}, u32[]{:S(2)}) %collective-permute-start) | collective-permute-done | bytes 196640 | tf_op jit(solution)/shard_map/while/body/eval_jaxpr/ppermute | solution.py:15
  171.4 18.3 %conditional.4 = (bf16[16,6144]{1,0:T(8,128)(2,1)}) conditional(s32[]{:T(128)} %convert_element_type.82, () %tuple.59, (pred[]{:T(512)}, s32[]{:T(128)}, bf16[8,16,6144]{2,1,0:T(8,128)(2,1)}, bf16[16,6144]{1,0:T(8,128)(2,1)S(1)}, f32[6144]{0:T(1024)}, /*index=5*/s32[384]{0:T(512)S(1)}, bf16[192,128,64]{1,2,0:T(8,128)(2,1)}, s32[192]{0:T(256)S(1)}, ...), branch_computations={%region_4.4_spmd, %region_5.6_spmd} | conditional | flops 78352080 | bytes 19506548 | solution.py:72
  180.4 3.9 %fusion.7 = bf16[16,192,64]{2,0,1:T(8,128)(2,1)S(1)} fusion(bf16[192,128,64]{1,2,0:T(8,128)(2,1)} %get-tuple-element.325, bf16[16,192,128]{2,1,0:T(8,128)(2,1)} %reshape.66), kind=kOutput, calls=%fused_computation.15 | convolution fusion | flops 52101120 | bytes 4325376 | tf_op jit(solution)/shard_map/while/body/eval_jaxpr/cond/branch_1_fun/ncr,crj->ncj/dot_general | solution.py:34
  197.5 18.3 %conditional.4 = (bf16[16,6144]{1,0:T(8,128)(2,1)}) conditional(s32[]{:T(128)} %convert_element_type.82, () %tuple.59, (pred[]{:T(512)}, s32[]{:T(128)}, bf16[8,16,6144]{2,1,0:T(8,128)(2,1)}, bf16[16,6144]{1,0:T(8,128)(2,1)S(1)}, f32[6144]{0:T(1024)}, /*index=5*/s32[384]{0:T(512)S(1)}, bf16[192,128,64]{1,2,0:T(8,128)(2,1)}, s32[192]{0:T(256)S(1)}, ...), branch_computations={%region_4.4_spmd, %region_5.6_spmd} | conditional | flops 78352080 | bytes 19506548 | solution.py:72
  206.5 3.9 %fusion.7 = bf16[16,192,64]{2,0,1:T(8,128)(2,1)S(1)} fusion(bf16[192,128,64]{1,2,0:T(8,128)(2,1)} %get-tuple-element.325, bf16[16,192,128]{2,1,0:T(8,128)(2,1)} %reshape.66), kind=kOutput, calls=%fused_computation.15 | convolution fusion | flops 52101120 | bytes 4325376 | tf_op jit(solution)/shard_map/while/body/eval_jaxpr/cond/branch_1_fun/ncr,crj->ncj/dot_general | solution.py:34
  223.6 18.3 %conditional.4 = (bf16[16,6144]{1,0:T(8,128)(2,1)}) conditional(s32[]{:T(128)} %convert_element_type.82, () %tuple.59, (pred[]{:T(512)}, s32[]{:T(128)}, bf16[8,16,6144]{2,1,0:T(8,128)(2,1)}, bf16[16,6144]{1,0:T(8,128)(2,1)S(1)}, f32[6144]{0:T(1024)}, /*index=5*/s32[384]{0:T(512)S(1)}, bf16[192,128,64]{1,2,0:T(8,128)(2,1)}, s32[192]{0:T(256)S(1)}, ...), branch_computations={%region_4.4_spmd, %region_5.6_spmd} | conditional | flops 78352080 | bytes 19506548 | solution.py:72
  232.6 3.9 %fusion.7 = bf16[16,192,64]{2,0,1:T(8,128)(2,1)S(1)} fusion(bf16[192,128,64]{1,2,0:T(8,128)(2,1)} %get-tuple-element.325, bf16[16,192,128]{2,1,0:T(8,128)(2,1)} %reshape.66), kind=kOutput, calls=%fused_computation.15 | convolution fusion | flops 52101120 | bytes 4325376 | tf_op jit(solution)/shard_map/while/body/eval_jaxpr/cond/branch_1_fun/ncr,crj->ncj/dot_general | solution.py:34
  249.6 18.3 %conditional.4 = (bf16[16,6144]{1,0:T(8,128)(2,1)}) conditional(s32[]{:T(128)} %convert_element_type.82, () %tuple.59, (pred[]{:T(512)}, s32[]{:T(128)}, bf16[8,16,6144]{2,1,0:T(8,128)(2,1)}, bf16[16,6144]{1,0:T(8,128)(2,1)S(1)}, f32[6144]{0:T(1024)}, /*index=5*/s32[384]{0:T(512)S(1)}, bf16[192,128,64]{1,2,0:T(8,128)(2,1)}, s32[192]{0:T(256)S(1)}, ...), branch_computations={%region_4.4_spmd, %region_5.6_spmd} | conditional | flops 78352080 | bytes 19506548 | solution.py:72
  258.7 3.9 %fusion.7 = bf16[16,192,64]{2,0,1:T(8,128)(2,1)S(1)} fusion(bf16[192,128,64]{1,2,0:T(8,128)(2,1)} %get-tuple-element.325, bf16[16,192,128]{2,1,0:T(8,128)(2,1)} %reshape.66), kind=kOutput, calls=%fused_computation.15 | convolution fusion | flops 52101120 | bytes 4325376 | tf_op jit(solution)/shard_map/while/body/eval_jaxpr/cond/branch_1_fun/ncr,crj->ncj/dot_general | solution.py:34
  275.7 18.3 %conditional.4 = (bf16[16,6144]{1,0:T(8,128)(2,1)}) conditional(s32[]{:T(128)} %convert_element_type.82, () %tuple.59, (pred[]{:T(512)}, s32[]{:T(128)}, bf16[8,16,6144]{2,1,0:T(8,128)(2,1)}, bf16[16,6144]{1,0:T(8,128)(2,1)S(1)}, f32[6144]{0:T(1024)}, /*index=5*/s32[384]{0:T(512)S(1)}, bf16[192,128,64]{1,2,0:T(8,128)(2,1)}, s32[192]{0:T(256)S(1)}, ...), branch_computations={%region_4.4_spmd, %region_5.6_spmd} | conditional | flops 78352080 | bytes 19506548 | solution.py:72
  301.8 18.3 %conditional.4 = (bf16[16,6144]{1,0:T(8,128)(2,1)}) conditional(s32[]{:T(128)} %convert_element_type.82, () %tuple.59, (pred[]{:T(512)}, s32[]{:T(128)}, bf16[8,16,6144]{2,1,0:T(8,128)(2,1)}, bf16[16,6144]{1,0:T(8,128)(2,1)S(1)}, f32[6144]{0:T(1024)}, /*index=5*/s32[384]{0:T(512)S(1)}, bf16[192,128,64]{1,2,0:T(8,128)(2,1)}, s32[192]{0:T(256)S(1)}, ...), branch_computations={%region_4.4_spmd, %region_5.6_spmd} | conditional | flops 78352080 | bytes 19506548 | solution.py:72
  330.2 37.9 %conditional.2 = (bf16[16,6144]{1,0:T(8,128)(2,1)}) conditional(s32[]{:T(128)} %convert_element_type.51, () %tuple.41, (pred[]{:T(512)}, bf16[128,6144]{1,0:T(8,128)(2,1)}, bf16[16,6144]{1,0:T(8,128)(2,1)}, f32[6144]{0:T(1024)}, s32[384]{0:T(512)S(1)}, /*index=5*/bf16[192,128,64]{2,1,0:T(8,128)(2,1)}, s32[192]{0:T(256)S(1)}, ...), branch_computations={%region_8.9_spmd, %region_9.11_spmd} | conditional | flops 78352080 | bytes 18720036 | solution.py:72
  347.1 5.7 %fusion.21 = bf16[16,192,64]{2,0,1:T(8,128)(2,1)} fusion(bf16[192,128,64]{2,1,0:T(8,128)(2,1)} %get-tuple-element.387, bf16[16,192,128]{2,1,0:T(8,128)(2,1)} %reshape.70), kind=kOutput, calls=%fused_computation.43 | convolution fusion | flops 52101120 | bytes 4325376 | tf_op jit(solution)/shard_map/cond/branch_1_fun/ncr,crj->ncj/dot_general | solution.py:34
  (260 shorter events, 215.5 us)
Async XLA Ops:
  6.5 3.2 copy-start.8
  6.5 1.6 copy-start.6
  6.5 49.6 %all-gather.5.cloned.1.call-start = ((), (), s32[]{:S(2)}) async-start(), calls=%async_computation.1 | async-start | bytes 3342336 | tf_op jit(solution)/shard_map/all_gather | solution.py:48
  9.0 93.4 %all-gather.3.cloned.1.call-start = ((), (), s32[]{:S(2)}) async-start(), calls=%async_computation | async-start | bytes 3342336 | tf_op jit(solution)/shard_map/all_gather | solution.py:47
  15.1 2.8 copy-start.9
  15.1 3.0 copy-start.10
  15.1 3.3 copy-start.7
  119.5 25.0 %collective-permute-start = (bf16[16,6144]{1,0:T(8,128)(2,1)}, bf16[16,6144]{1,0:T(8,128)(2,1)S(1)}, u32[]{:S(2)}, u32[]{:S(2)}) collective-permute-start(bf16[16,6144]{1,0:T(8,128)(2,1)} %get-tuple-element.529), channel_id=1, source_target_pairs={{0,16},{1,17},{2,18},{3,19},{4,20},{5,21},{6,22},{7,23},{8,24},{9,... | collective-permute-start | bytes 589832 | tf_op jit(solution)/shard_map/while/body/eval_jaxpr/ppermute | solution.py:15
  161.1 0.9 copy-start.2
  162.8 8.7 %collective-permute-start = (bf16[16,6144]{1,0:T(8,128)(2,1)}, bf16[16,6144]{1,0:T(8,128)(2,1)S(1)}, u32[]{:S(2)}, u32[]{:S(2)}) collective-permute-start(bf16[16,6144]{1,0:T(8,128)(2,1)} %get-tuple-element.529), channel_id=1, source_target_pairs={{0,16},{1,17},{2,18},{3,19},{4,20},{5,21},{6,22},{7,23},{8,24},{9,... | collective-permute-start | bytes 589832 | tf_op jit(solution)/shard_map/while/body/eval_jaxpr/ppermute | solution.py:15
  188.0 0.9 copy-start.2
  189.7 7.8 %collective-permute-start = (bf16[16,6144]{1,0:T(8,128)(2,1)}, bf16[16,6144]{1,0:T(8,128)(2,1)S(1)}, u32[]{:S(2)}, u32[]{:S(2)}) collective-permute-start(bf16[16,6144]{1,0:T(8,128)(2,1)} %get-tuple-element.529), channel_id=1, source_target_pairs={{0,16},{1,17},{2,18},{3,19},{4,20},{5,21},{6,22},{7,23},{8,24},{9,... | collective-permute-start | bytes 589832 | tf_op jit(solution)/shard_map/while/body/eval_jaxpr/ppermute | solution.py:15
  214.1 0.9 copy-start.2
  215.8 7.8 %collective-permute-start = (bf16[16,6144]{1,0:T(8,128)(2,1)}, bf16[16,6144]{1,0:T(8,128)(2,1)S(1)}, u32[]{:S(2)}, u32[]{:S(2)}) collective-permute-start(bf16[16,6144]{1,0:T(8,128)(2,1)} %get-tuple-element.529), channel_id=1, source_target_pairs={{0,16},{1,17},{2,18},{3,19},{4,20},{5,21},{6,22},{7,23},{8,24},{9,... | collective-permute-start | bytes 589832 | tf_op jit(solution)/shard_map/while/body/eval_jaxpr/ppermute | solution.py:15
  240.2 0.9 copy-start.2
  241.9 7.8 %collective-permute-start = (bf16[16,6144]{1,0:T(8,128)(2,1)}, bf16[16,6144]{1,0:T(8,128)(2,1)S(1)}, u32[]{:S(2)}, u32[]{:S(2)}) collective-permute-start(bf16[16,6144]{1,0:T(8,128)(2,1)} %get-tuple-element.529), channel_id=1, source_target_pairs={{0,16},{1,17},{2,18},{3,19},{4,20},{5,21},{6,22},{7,23},{8,24},{9,... | collective-permute-start | bytes 589832 | tf_op jit(solution)/shard_map/while/body/eval_jaxpr/ppermute | solution.py:15
  266.3 0.9 copy-start.2
  268.0 7.8 %collective-permute-start = (bf16[16,6144]{1,0:T(8,128)(2,1)}, bf16[16,6144]{1,0:T(8,128)(2,1)S(1)}, u32[]{:S(2)}, u32[]{:S(2)}) collective-permute-start(bf16[16,6144]{1,0:T(8,128)(2,1)} %get-tuple-element.529), channel_id=1, source_target_pairs={{0,16},{1,17},{2,18},{3,19},{4,20},{5,21},{6,22},{7,23},{8,24},{9,... | collective-permute-start | bytes 589832 | tf_op jit(solution)/shard_map/while/body/eval_jaxpr/ppermute | solution.py:15
  292.4 0.9 copy-start.2
  294.0 7.8 %collective-permute-start = (bf16[16,6144]{1,0:T(8,128)(2,1)}, bf16[16,6144]{1,0:T(8,128)(2,1)S(1)}, u32[]{:S(2)}, u32[]{:S(2)}) collective-permute-start(bf16[16,6144]{1,0:T(8,128)(2,1)} %get-tuple-element.529), channel_id=1, source_target_pairs={{0,16},{1,17},{2,18},{3,19},{4,20},{5,21},{6,22},{7,23},{8,24},{9,... | collective-permute-start | bytes 589832 | tf_op jit(solution)/shard_map/while/body/eval_jaxpr/ppermute | solution.py:15
  318.4 0.9 copy-start.2
  320.1 7.8 %collective-permute-start = (bf16[16,6144]{1,0:T(8,128)(2,1)}, bf16[16,6144]{1,0:T(8,128)(2,1)S(1)}, u32[]{:S(2)}, u32[]{:S(2)}) collective-permute-start(bf16[16,6144]{1,0:T(8,128)(2,1)} %get-tuple-element.529), channel_id=1, source_target_pairs={{0,16},{1,17},{2,18},{3,19},{4,20},{5,21},{6,22},{7,23},{8,24},{9,... | collective-permute-start | bytes 589832 | tf_op jit(solution)/shard_map/while/body/eval_jaxpr/ppermute | solution.py:15
  330.2 37.9 %copy-start.3 = (bf16[8,16,6144]{2,1,0:T(8,128)(2,1)S(1)}, bf16[8,16,6144]{2,1,0:T(8,128)(2,1)}, u32[]{:S(2)}) copy-start(bf16[8,16,6144]{2,1,0:T(8,128)(2,1)} %get-tuple-element.350) | copy-start | bytes 4718596
  372.8 1.3 copy-start
  (9 other events, 6.1 us)
Sparse Core Ops, SparseCore 0:
  9.6 46.4 all-gather.4
  58.4 43.9 all-gather.2
where the time goes:
time: 384 us; the launch traced here: 381 us
  local copies, waits for them, and re-layouts  142 us (37%)
  waiting for transfers between devices  112 us (29%)
  matrix products  52.2 us (14%)
  other arithmetic  50.4 us (13%)
  between operations  13.5 us (4%)
  starting transfers between devices  10.3 us (3%)
    ppermute x8, waiting for transfers between devices, from_behind(): lax.ppermute(value, axis, [(source, source + steps) for source in range(i...  49.9 us
    all_gather x1, waiting for transfers between devices, per_device(): lax.all_gather(down_blocks, 'fsdp', axis=1, tiled=True)  37.1 us
    gather x16, local copies, waits for them, and re-layouts, layer(): picked = normed.reshape(count, blocks_in, BLK)[:, up_index, :]  36.5 us
    dot_general x8, matrix products, layer(): jnp.einsum('ncr,crj->ncj', picked, weights_up, preferred_element_type=jnp...  33 us
    all_gather x1, waiting for transfers between devices, per_device(): lax.all_gather(up_blocks, 'fsdp', axis=1, tiled=True)  24.2 us
    dot_general x8, matrix products, layer(): jnp.einsum('ncr,crj->ncj', second, weights_down, preferred_element_type=j...  19.2 us
    reshape x8, local copies, waits for them, and re-layouts, layer(): picked = picked.reshape(count, blocks_hid, UP_DEPTH * BLK)  13.8 us
    dynamic_update_slice x9, other arithmetic, advance(): record = lax.dynamic_update_index_in_dim(record, updated, slot, 0)  13.4 us
  transfers between devices with their start and end apart: 10, of which 10 were waited for; matrix products, arithmetic and copies ran while one was open for 13% of the time, Pallas kernels for 0%

commit v1 on v0

v1 whole, which is shorter than its diff:
```python
import functools
import jax
import jax.numpy as jnp
from jax import lax
from jax.experimental import pallas as pl
from jax.experimental.pallas import tpu as pltpu
from jax.sharding import PartitionSpec as P

BLK = 64
UP_DEPTH = 2
DOWN_DEPTH = 2


def project(source, index, weights):
    count = source.shape[0]

    def one(column, sums):
        first = lax.dynamic_slice_in_dim(source, index[2 * column] * BLK, BLK, 1)
        second = lax.dynamic_slice_in_dim(source, index[2 * column + 1] * BLK, BLK, 1)
        part = jnp.dot(
            jnp.concatenate([first, second], axis=1),
            lax.dynamic_index_in_dim(weights, column, 0, keepdims=False),
            preferred_element_type=jnp.float32,
        )
        return lax.dynamic_update_slice_in_dim(sums, part, column * BLK, 1)

    columns = weights.shape[0]
    return lax.fori_loop(0, columns, one, jnp.zeros((count, columns * BLK), jnp.float32))


def per_device(activations, keep, gains, up_rows, up_blocks, down_rows, down_blocks):
    up_all = lax.all_gather(up_blocks[0], "fsdp", axis=0, tiled=True)
    down_all = lax.all_gather(down_blocks[0], "fsdp", axis=0, tiled=True)
    weights_up = up_all.reshape(-1, UP_DEPTH * BLK, BLK)
    weights_down = down_all.reshape(-1, DOWN_DEPTH * BLK, BLK)
    gain_wide = gains[0].astype(jnp.float32)
    keep_wide = keep.astype(jnp.float32)[:, None]
    section = lax.axis_index("section")
    sections = lax.axis_size("section")

    def turn_step(turn, carry):
        held, record = carry
        wide = held.astype(jnp.float32)
        meansq = jnp.mean(wide * wide, axis=-1, keepdims=True)
        normed = (wide * lax.rsqrt(meansq + 1e-05) * gain_wide).astype(jnp.bfloat16)
        up_sums = project(normed, up_rows[0].reshape(-1), weights_up)
        hidden = jax.nn.gelu(up_sums, approximate=True).astype(jnp.bfloat16)
        down_sums = project(hidden, down_rows[0].reshape(-1), weights_down)
        result = (wide + keep_wide * down_sums).astype(jnp.bfloat16)
        record = jnp.where(section == turn, result, record)
        pairs = [(source, source + 1) for source in range(sections - 1)]
        return lax.ppermute(result, "section", pairs), record

    return lax.fori_loop(0, sections, turn_step, (activations, activations))[1][None]


LANES = 2 * BLK
MESH = pl.DeviceIdType.MESH
RING, SIB, ACROSS = 0, 1, 2


def kernel(
    chips,
    x_ref,
    keep_ref,
    gain_ref,
    rows_ref,
    w_ref,
    out_ref,
    weights,
    blocks_in,
    blocks_hid,
    scale_ref,
    gains,
    rows_in,
    rows,
    send_sem,
    recv_sem,
    small_send,
    small_recv,
    local_sem,
):
    section = lax.axis_index("section")
    me = lax.axis_index("fsdp")
    core = me % 2
    chip = me // 2
    depth_z = chips // 2
    y = chip % 2
    z = chip // 2
    place = z * (1 - y) + (chips - 1 - z) * y
    step_dir = 1 - 2 * core

    def at(position, which):
        position = (position + 2 * chips) % chips
        back = position // depth_z
        zz = position * (1 - back) + (chips - 1 - position) * back
        return (zz * 2 + back) * 2 + which

    ahead = at(place + step_dir, core)
    behind = at(place - step_dir, core)
    sibling = me + 1 - 2 * core
    other = 1 - section
    tokens, width = x_ref.shape
    tiles = width // LANES
    ups = 6 * w_ref.shape[0] // 9
    part = w_ref.shape[0] // 3

    barrier = pltpu.get_barrier_semaphore()
    for device in ((section, ahead), (section, behind), (section, sibling), (other, me)):
        pl.semaphore_signal(barrier, inc=1, device_id=device, device_id_type=MESH)
    pl.semaphore_wait(barrier, 4)

    def origin(step):
        return at(place - step_dir * step, core)

    def origin_sib(step):
        return at(place + step_dir * step, 1 - core)

    def slot(layer, who, piece):
        return weights.at[layer, who, pl.ds(piece * part, part)]

    def send(layer, step, piece, way, own=False):
        who = origin(step)
        device = ((section, ahead), (section, sibling), (other, me))[way]
        return pltpu.make_async_remote_copy(
            src_ref=w_ref.at[pl.ds(piece * part, part)] if own else slot(layer, who, piece),
            dst_ref=slot(layer, who, piece),
            send_sem=send_sem.at[layer, step, piece, way],
            recv_sem=recv_sem.at[layer, who, piece],
            device_id=device,
            device_id_type=MESH,
        )

    def arrive(layer, who, piece):
        pltpu.make_async_remote_copy(
            src_ref=slot(layer, who, piece),
            dst_ref=slot(layer, who, piece),
            send_sem=send_sem.at[layer, 0, piece, RING],
            recv_sem=recv_sem.at[layer, who, piece],
            device_id=(section, sibling),
            device_id_type=MESH,
        ).wait_recv()

    def small(index):
        return pltpu.make_async_remote_copy(
            src_ref=(gain_ref, rows_ref)[index],
            dst_ref=(gains.at[0], rows_in)[index],
            send_sem=small_send.at[index],
            recv_sem=small_recv.at[index],
            device_id=(other, me),
            device_id_type=MESH,
        )

    @pl.when(section == 0)
    def _():
        small(0).start()
        small(1).start()
        send(0, 0, 2, ACROSS, True).start()
        for piece in range(3):
            send(0, 0, piece, RING, True).start()
        for piece in range(2):
            send(0, 0, piece, ACROSS, True).start()
        for piece in range(3):
            send(0, 0, piece, SIB, True).start()
        gains[0] = gain_ref[...]
        weights[0, me] = w_ref[...]
        own = pltpu.make_async_copy(rows_ref, rows.at[0], local_sem.at[0])
        own.start()
        own.wait()

    @pl.when(section == 1)
    def _():
        for piece in range(3):
            send(1, 0, piece, RING, True).start()
        for piece in range(3):
            send(1, 0, piece, SIB, True).start()
        gains[1] = gain_ref[...]
        weights[1, me] = w_ref[...]
        own = pltpu.make_async_copy(rows_ref, rows.at[1], local_sem.at[0])
        own.start()
        small(0).wait_recv()
        small(1).wait_recv()
        own.wait()
        first = pltpu.make_async_copy(rows_in, rows.at[0], local_sem.at[1])
        first.start()
        first.wait()
        arrive(0, me, 2)
        send(0, 0, 2, RING).start()
        send(0, 0, 2, SIB).start()

    low = lax.broadcasted_iota(jnp.int32, (tokens, LANES), 1) < BLK
    low_w = lax.broadcasted_iota(jnp.int32, (LANES, LANES), 1) < BLK

    def both(target, tile, value):
        target[2 * tile] = value.astype(jnp.bfloat16)
        target[2 * tile + 1] = pltpu.roll(value, BLK, 1).astype(jnp.bfloat16)

    def norm(layer, source):
        def square(tile, total):
            wide = source[:, pl.ds(pl.multiple_of(tile * LANES, LANES), LANES)].astype(jnp.float32)
            return total + wide * wide

        total = lax.fori_loop(0, tiles, square, jnp.zeros((tokens, LANES), jnp.float32))
        mean = jnp.sum(total, axis=1, keepdims=True) * (1.0 / width)
        scale_ref[...] = jnp.broadcast_to(lax.rsqrt(mean + 1e-05), (tokens, LANES))

        def apply(tile, _):
            columns = pl.ds(pl.multiple_of(tile * LANES, LANES), LANES)
            wide = source[:, columns].astype(jnp.float32)
            both(blocks_in, tile, wide * scale_ref[...] * gains[layer, :, columns])
            return 0

        lax.fori_loop(0, tiles, apply, 0, unroll=2)

    def product(layer, source, base, pair, who, local):
        picked, kernels = [], []
        value = weights[layer, who, local]
        zero = jnp.zeros_like(value)
        for half in range(2):
            place_a = base + pair * 4 + half * 2
            index_a = rows[layer, place_a // 128, place_a % 128]
            index_b = rows[layer, (place_a + 1) // 128, (place_a + 1) % 128]
            picked.append(jnp.where(low, source[index_a], source[index_b]))
            kernels.append(jnp.where(low_w, value, zero) if half == 0 else jnp.where(low_w, zero, value))
        return jnp.dot(
            jnp.concatenate(picked, axis=1),
            jnp.concatenate(kernels, axis=0),
            preferred_element_type=jnp.float32,
        )

    def up(layer, who):
        def one(local, _):
            pair = who * ups + local
            sums = product(layer, blocks_in, 0, pair, who, local)
            both(blocks_hid, pair, jax.nn.gelu(sums, approximate=True))
            return 0

        lax.fori_loop(0, ups, one, 0, unroll=2)

    def down(layer, source):
        def one(who, _):
            for local in range(part):
                tile = who * part + local
                sums = product(layer, blocks_hid, 4 * ups * 2 * chips, tile, who, ups + local)
                columns = pl.ds(pl.multiple_of(tile * LANES, LANES), LANES)
                wide = source[:, columns].astype(jnp.float32)
                out_ref[:, columns] = (wide + keep_ref[...] * sums).astype(jnp.bfloat16)
            return 0

        lax.fori_loop(0, 2 * chips, one, 0)

    norm(0, x_ref)

    def step(s, _):
        @pl.when(section == 0)
        def _():
            @pl.when(s > 0)
            def _():
                for piece in range(3):
                    arrive(0, origin(s), piece)

                    @pl.when(s < chips - 1)
                    def _():
                        send(0, s, piece, RING).start()

                    if piece < 2:
                        send(0, s, piece, ACROSS).start()
                    send(0, s, piece, SIB).start()

        @pl.when(section == 1)
        def _():
            @pl.when(s > 0)
            def _():
                for layer, piece in ((1, 0), (1, 1), (1, 2), (0, 2)):
                    arrive(layer, origin(s), piece)

                    @pl.when(s < chips - 1)
                    def _():
                        send(layer, s, piece, RING).start()

                    send(layer, s, piece, SIB).start()

            for piece in range(2):
                arrive(0, origin(s), piece)
                send(0, s, piece, SIB).start()

        up(0, origin(s))

        @pl.when(s > 0)
        def _():
            for piece in range(2):
                arrive(0, origin_sib(s - 1), piece)
            up(0, origin_sib(s - 1))

        return 0

    lax.fori_loop(0, chips, step, 0)
    for piece in range(2):
        arrive(0, origin_sib(chips - 1), piece)
    up(0, origin_sib(chips - 1))

    def rest(s, _):
        arrive(0, origin_sib(s), 2)
        return 0

    lax.fori_loop(0, chips, rest, 0)
    down(0, x_ref)

    @pl.when(section == 1)
    def _():
        norm(1, out_ref)

        def one(s, _):
            for piece in range(3):
                arrive(1, origin_sib(s), piece)
            up(1, origin(s))
            up(1, origin_sib(s))
            return 0

        lax.fori_loop(0, chips, one, 0)
        down(1, out_ref)

    def finish(s, _):
        @pl.when(section == 0)
        def _():
            for piece in range(3):
                @pl.when(s < chips - 1)
                def _():
                    send(0, s, piece, RING).wait_send()

                if piece < 2:
                    send(0, s, piece, ACROSS).wait_send()
                send(0, s, piece, SIB).wait_send()

        @pl.when(section == 1)
        def _():
            for layer, piece in ((1, 0), (1, 1), (1, 2), (0, 2)):
                @pl.when(s < chips - 1)
                def _():
                    send(layer, s, piece, RING).wait_send()

                send(layer, s, piece, SIB).wait_send()
            for piece in range(2):
                send(0, s, piece, SIB).wait_send()

        return 0

    lax.fori_loop(0, chips, finish, 0)

    @pl.when(section == 0)
    def _():
        send(0, 0, 2, ACROSS).wait_send()
        small(0).wait_send()
        small(1).wait_send()


def paired(values, count):
    pairs = values.shape[0] // 4
    return values.reshape(pairs, 2, LANES, BLK).transpose(0, 2, 1, 3).reshape(pairs, LANES, LANES)


def flat_rows(index, depth):
    return jnp.stack([index[:, 0], index[:, 1] ^ 1], axis=1).reshape(-1)


def per_device_fused(activations, keep, gains, up_rows, up_blocks, down_rows, down_blocks):
    tokens, width = activations.shape
    devices = lax.axis_size("fsdp")
    own = jnp.concatenate([paired(up_blocks[0], UP_DEPTH), paired(down_blocks[0], DOWN_DEPTH)], axis=0)
    table = jnp.concatenate([flat_rows(up_rows[0], UP_DEPTH), flat_rows(down_rows[0], DOWN_DEPTH)])
    table = jnp.pad(table, (0, 1024 - table.shape[0])).reshape(8, 128)
    keep_wide = jnp.broadcast_to(keep.astype(jnp.float32)[:, None], (tokens, LANES))
    vmem = pl.BlockSpec(memory_space=pltpu.VMEM)
    result = pl.pallas_call(
        functools.partial(kernel, devices // 2),
        out_shape=jax.ShapeDtypeStruct((tokens, width), jnp.bfloat16),
        in_specs=[vmem] * 5,
        out_specs=vmem,
        scratch_shapes=[
            pltpu.VMEM((2, devices) + own.shape, jnp.bfloat16),
            pltpu.VMEM((width // BLK, tokens, LANES), jnp.bfloat16),
            pltpu.VMEM((up_rows.shape[1], tokens, LANES), jnp.bfloat16),
            pltpu.VMEM((tokens, LANES), jnp.float32),
            pltpu.VMEM((2, 1, width), jnp.float32),
            pltpu.VMEM((8, 128), jnp.int32),
            pltpu.SMEM((2, 8, 128), jnp.int32),
            pltpu.SemaphoreType.DMA((2, devices // 2, 3, 3)),
            pltpu.SemaphoreType.DMA((2, devices, 3)),
            pltpu.SemaphoreType.DMA((2,)),
            pltpu.SemaphoreType.DMA((2,)),
            pltpu.SemaphoreType.DMA((2,)),
        ],
        compiler_params=pltpu.CompilerParams(
            collective_id=0, has_side_effects=True, vmem_limit_bytes=48 * 1024 * 1024
        ),
    )(activations, keep_wide, gains.astype(jnp.float32), table, own)
    return result[None]


def solution(mesh):
    fused = mesh.shape["section"] == 2 and mesh.shape["fsdp"] == 16
    return jax.shard_map(
        per_device_fused if fused else per_device,
        mesh=mesh,
        in_specs=(
            P("fsdp", None),
            P("fsdp"),
            P("section", None),
            P("section", None, None),
            P("section", "fsdp", None),
            P("section", None, None),
            P("section", "fsdp", None),
        ),
        out_specs=P("section", "fsdp", None),
        check_vma=False,
    )
```

time: 384 us -> 84.7 us (0.22)
  local copies, waits for them, and re-layouts: 142 us -> 4.97 us
  waiting for transfers between devices: 112 us -> 0 us
  Pallas kernels: 0 us -> 76.2 us
  matrix products: 52.2 us -> 0 us
  other arithmetic: 50.4 us -> 3.17 us
  between operations: 13.5 us -> 0.09 us
  starting transfers between devices: 10.3 us -> 0 us
    pallas_call x0 -> x1, Pallas kernels: none -> 76.2 us  [per_device_fused(): pl.pallas_call(functools.partial(kernel, devices // 2), out_shape=jax.Sha...]
    all_gather x2 -> x0, waiting for transfers between devices: 61.2 us -> none  [the longest x1 37.1 us: per_device(): lax.all_gather(down_blocks, 'fsdp', axis=1, tiled=True)]
    dot_general x16 -> x0, matrix products: 52.2 us -> none  [the longest x8 33 us: layer(): jnp.einsum('ncr,crj->ncj', picked, weights_up, preferred_element_type=jnp...]
    gather x33 -> x0, local copies, waits for them, and re-layouts: 51 us -> none  [the longest x16 36.5 us: layer(): picked = normed.reshape(count, blocks_in, BLK)[:, up_index, :]]
    ppermute x8 -> x0, waiting for transfers between devices: 49.9 us -> none  [from_behind(): lax.ppermute(value, axis, [(source, source + steps) for source in range(i...]
    reshape x41 -> x5, local copies, waits for them, and re-layouts: 30.3 us -> 0.59 us  [the longest x2 0.31 us: paired(): values.reshape(pairs, 2, LANES, BLK).transpose(0, 2, 1, 3)]
    another operation x6 -> x4, local copies, waits for them, and re-layouts: 16.3 us -> 2.69 us  [the longest x2 2.47 us: paired(): values.reshape(pairs, 2, LANES, BLK).transpose(0, 2, 1, 3)]
    dynamic_update_slice x9 -> x0, other arithmetic: 13.4 us -> none  [advance(): record = lax.dynamic_update_index_in_dim(record, updated, slot, 0)]
  transfers between devices with their start and end apart: 10 -> 0, of which waited for: 10 -> 0; matrix products, arithmetic and copies ran while one was open for 13% -> 0% of each run, Pallas kernels for 0% -> 0%
where the time goes in v1:
time: 84.7 us; the launch traced here: 84.4 us
  Pallas kernels  76.2 us (90%)
  local copies, waits for them, and re-layouts  4.97 us (6%)
  other arithmetic  3.17 us (4%)
    pallas_call x1, Pallas kernels, per_device_fused(): pl.pallas_call(functools.partial(kernel, devices // 2), out_shape=jax.Sha...  76.2 us
    another operation x2, local copies, waits for them, and re-layouts, paired(): values.reshape(pairs, 2, LANES, BLK).transpose(0, 2, 1, 3)  2.47 us

profile of v1, /device:TPU:2, one launch (start us, length us, event | category | flops | bytes accessed | tf_op | source)
XLA Modules:
  0.0 84.4 jit_solution(11870826310816358858)
XLA Ops:
  0.0 0.0 copy-start
  0.0 0.8 convert_element_type.6
  0.8 0.8 fusion.1
  1.6 0.8 fusion
  2.4 0.8 convert_element_type.7.gain_ref
  3.1 0.1 copy.11
  3.2 0.1 reshape.17
  3.4 0.1 broadcast_in_dim.4.keep_ref
  3.5 0.1 copy.10
  3.6 0.1 reshape.16
  3.8 1.1 %reshape_squeeze.7 = bf16[3,2,128,64]{3,2,1,0:T(8,128)(2,1)S(1)} reshape(bf16[1,12,4096]{2,1,0:T(8,128)(2,1)} %param.13) | data formatting | bytes 196608 | tf_op jit(solution)/shard_map/reshape;squeeze | solution.py:359
  4.9 0.1 copy.13
  5.1 0.1 copy.15
  5.2 1.3 %reshape_squeeze.6 = bf16[6,2,128,64]{3,2,1,0:T(8,128)(2,1)S(1)} reshape(bf16[1,24,4096]{2,1,0:T(8,128)(2,1)} %param.11) | data formatting | bytes 393216 | tf_op jit(solution)/shard_map/reshape;squeeze | solution.py:359
  6.5 0.2 copy.12
  6.7 0.2 copy.14
  6.9 0.0 copy-done
  6.9 76.2 %shard_map.73 = bf16[160,6144]{1,0:T(8,128)(2,1)S(1)} custom-call(bf16[160,6144]{1,0:T(8,128)(2,1)S(1)} %copy-done, f32[160,128]{1,0:T(8,128)S(1)} %broadcast_in_dim.4.keep_ref, f32[1,6144]{1,0:T(1,128)S(1)} %convert_element_type.7.gain_ref, s32[8,128]{1,0:T(8,128)S(1)} %pad_bitcast_fusion.rows_ref, bf16[9,128,128]{2,1,0:T(8,128)(2,1)S(1)} %pad_maximum_fusion.w_ref), custom_call_target="tpu_custom_call" | custom-call | tf_op jit(solution)/shard_map/pallas_call | solution.py:374
  83.2 1.3 %copy.17 = bf16[1,160,6144]{2,1,0:T(8,128)(2,1)} copy(bf16[1,160,6144]{2,1,0:T(8,128)(2,1)S(1)} %bitcast.9) | data formatting | bytes 3932160
  (5 shorter events, 0.1 us)
Async XLA Ops:
  0.0 6.9 %copy-start = (bf16[160,6144]{1,0:T(8,128)(2,1)S(1)}, bf16[160,6144]{1,0:T(8,128)(2,1)}, u32[]{:S(2)}) copy-start(bf16[160,6144]{1,0:T(8,128)(2,1)} %x_ref.1) | copy-start | bytes 5898244

commit v2 on v1

--- a/solution.py
+++ b/solution.py
@@ -62,7 +62,7 @@
 def kernel(
     chips,
     x_ref,
-    keep_ref,
+    keep_row,
     gain_ref,
     rows_ref,
     w_ref,
@@ -71,6 +71,7 @@
     blocks_in,
     blocks_hid,
     scale_ref,
+    keep_ref,
     gains,
     rows_in,
     rows,
@@ -143,7 +144,7 @@
 
     def small(index):
         return pltpu.make_async_remote_copy(
-            src_ref=(gain_ref, rows_ref)[index],
+            src_ref=(gains.at[0], rows_ref)[index],
             dst_ref=(gains.at[0], rows_in)[index],
             send_sem=small_send.at[index],
             recv_sem=small_recv.at[index],
@@ -153,6 +154,7 @@
 
     @pl.when(section == 0)
     def _():
+        gains[0] = gain_ref[...].astype(jnp.float32)
         small(0).start()
         small(1).start()
         send(0, 0, 2, ACROSS, True).start()
@@ -162,7 +164,6 @@
             send(0, 0, piece, ACROSS, True).start()
         for piece in range(3):
             send(0, 0, piece, SIB, True).start()
-        gains[0] = gain_ref[...]
         weights[0, me] = w_ref[...]
         own = pltpu.make_async_copy(rows_ref, rows.at[0], local_sem.at[0])
         own.start()
@@ -174,7 +175,7 @@
             send(1, 0, piece, RING, True).start()
         for piece in range(3):
             send(1, 0, piece, SIB, True).start()
-        gains[1] = gain_ref[...]
+        gains[1] = gain_ref[...].astype(jnp.float32)
         weights[1, me] = w_ref[...]
         own = pltpu.make_async_copy(rows_ref, rows.at[1], local_sem.at[0])
         own.start()
@@ -188,19 +189,29 @@
         send(0, 0, 2, RING).start()
         send(0, 0, 2, SIB).start()
 
-    low = lax.broadcasted_iota(jnp.int32, (tokens, LANES), 1) < BLK
-    low_w = lax.broadcasted_iota(jnp.int32, (LANES, LANES), 1) < BLK
+    low = lax.broadcasted_iota(jnp.int32, (16, LANES), 1) < BLK
+
+    def merge(first, second):
+        shape = (first.shape[0] // 16, 16, LANES)
+        return jnp.where(low[None], first.reshape(shape), second.reshape(shape)).reshape(first.shape)
+
+
+    def gelu(value):
+        inner = value * (0.7978845608028654 + 0.035677408136300125 * (value * value))
+        scaled = 0.5 * value
+        return scaled + scaled * jnp.tanh(inner)
 
     def both(target, tile, value):
-        target[2 * tile] = value.astype(jnp.bfloat16)
-        target[2 * tile + 1] = pltpu.roll(value, BLK, 1).astype(jnp.bfloat16)
+        rounded = value.astype(jnp.bfloat16)
+        target[2 * tile] = rounded
+        target[2 * tile + 1] = jnp.concatenate([rounded[:, BLK:], rounded[:, :BLK]], axis=1)
 
     def norm(layer, source):
         def square(tile, total):
             wide = source[:, pl.ds(pl.multiple_of(tile * LANES, LANES), LANES)].astype(jnp.float32)
             return total + wide * wide
 
-        total = lax.fori_loop(0, tiles, square, jnp.zeros((tokens, LANES), jnp.float32))
+        total = lax.fori_loop(0, tiles, square, jnp.zeros((tokens, LANES), jnp.float32), unroll=8)
         mean = jnp.sum(total, axis=1, keepdims=True) * (1.0 / width)
         scale_ref[...] = jnp.broadcast_to(lax.rsqrt(mean + 1e-05), (tokens, LANES))
 
@@ -210,7 +221,7 @@
             both(blocks_in, tile, wide * scale_ref[...] * gains[layer, :, columns])
             return 0
 
-        lax.fori_loop(0, tiles, apply, 0, unroll=2)
+        lax.fori_loop(0, tiles, apply, 0, unroll=8)
 
     def product(layer, source, base, pair, who, local):
         picked, kernels = [], []
@@ -219,9 +230,9 @@
         for half in range(2):
             place_a = base + pair * 4 + half * 2
             index_a = rows[layer, place_a // 128, place_a % 128]
-            index_b = rows[layer, (place_a + 1) // 128, (place_a + 1) % 128]
-            picked.append(jnp.where(low, source[index_a], source[index_b]))
-            kernels.append(jnp.where(low_w, value, zero) if half == 0 else jnp.where(low_w, zero, value))
+            index_b = rows[layer, (place_a + 1) // 128, (place_a + 1) % 128] ^ 1
+            picked.append(merge(source[index_a], source[index_b]))
+            kernels.append(merge(value, zero) if half == 0 else merge(zero, value))
         return jnp.dot(
             jnp.concatenate(picked, axis=1),
             jnp.concatenate(kernels, axis=0),
@@ -232,10 +243,10 @@
         def one(local, _):
             pair = who * ups + local
             sums = product(layer, blocks_in, 0, pair, who, local)
-            both(blocks_hid, pair, jax.nn.gelu(sums, approximate=True))
+            both(blocks_hid, pair, gelu(sums))
             return 0
 
-        lax.fori_loop(0, ups, one, 0, unroll=2)
+        lax.fori_loop(0, ups, one, 0, unroll=6)
 
     def down(layer, source):
         def one(who, _):
@@ -247,8 +258,13 @@
                 out_ref[:, columns] = (wide + keep_ref[...] * sums).astype(jnp.bfloat16)
             return 0
 
-        lax.fori_loop(0, 2 * chips, one, 0)
-
+        lax.fori_loop(0, 2 * chips, one, 0, unroll=4)
+
+    same = lax.broadcasted_iota(jnp.int32, (tokens, tokens), 0) == lax.broadcasted_iota(
+        jnp.int32, (tokens, tokens), 1
+    )
+    kept = jnp.sum(jnp.where(same, keep_row[...].astype(jnp.float32), 0.0), axis=1, keepdims=True)
+    keep_ref[...] = jnp.broadcast_to(kept, (tokens, LANES))
     norm(0, x_ref)
 
     def step(s, _):
@@ -354,22 +370,17 @@
         small(1).wait_send()
 
 
-def paired(values, count):
+def paired(values):
     pairs = values.shape[0] // 4
     return values.reshape(pairs, 2, LANES, BLK).transpose(0, 2, 1, 3).reshape(pairs, LANES, LANES)
-
-
-def flat_rows(index, depth):
-    return jnp.stack([index[:, 0], index[:, 1] ^ 1], axis=1).reshape(-1)
 
 
 def per_device_fused(activations, keep, gains, up_rows, up_blocks, down_rows, down_blocks):
     tokens, width = activations.shape
     devices = lax.axis_size("fsdp")
-    own = jnp.concatenate([paired(up_blocks[0], UP_DEPTH), paired(down_blocks[0], DOWN_DEPTH)], axis=0)
-    table = jnp.concatenate([flat_rows(up_rows[0], UP_DEPTH), flat_rows(down_rows[0], DOWN_DEPTH)])
+    own = paired(jnp.concatenate([up_blocks[0], down_blocks[0]], axis=0))
+    table = jnp.concatenate([up_rows[0].reshape(-1), down_rows[0].reshape(-1)])
     table = jnp.pad(table, (0, 1024 - table.shape[0])).reshape(8, 128)
-    keep_wide = jnp.broadcast_to(keep.astype(jnp.float32)[:, None], (tokens, LANES))
     vmem = pl.BlockSpec(memory_space=pltpu.VMEM)
     result = pl.pallas_call(
         functools.partial(kernel, devices // 2),
@@ -380,6 +391,7 @@
             pltpu.VMEM((2, devices) + own.shape, jnp.bfloat16),
             pltpu.VMEM((width // BLK, tokens, LANES), jnp.bfloat16),
             pltpu.VMEM((up_rows.shape[1], tokens, LANES), jnp.bfloat16),
+            pltpu.VMEM((tokens, LANES), jnp.float32),
             pltpu.VMEM((tokens, LANES), jnp.float32),
             pltpu.VMEM((2, 1, width), jnp.float32),
             pltpu.VMEM((8, 128), jnp.int32),
@@ -393,7 +405,7 @@
         compiler_params=pltpu.CompilerParams(
             collective_id=0, has_side_effects=True, vmem_limit_bytes=48 * 1024 * 1024
         ),
-    )(activations, keep_wide, gains.astype(jnp.float32), table, own)
+    )(activations, keep[None], gains, table, own)
     return result[None]
 
 

time: 84.7 us -> 64.5 us (0.76)
  Pallas kernels: 76.2 us -> 58 us
  other arithmetic: 3.17 us -> 1.02 us
    pallas_call x1, Pallas kernels: 76.2 us -> 58 us  [per_device_fused(): pl.pallas_call(functools.partial(kernel, devices // 2), out_shape=jax.Sha...]
    another operation x4 -> x2, local copies, waits for them, and re-layouts: 2.69 us -> 0.28 us  [per_device_fused(): table = jnp.concatenate([up_rows[0].reshape(-1), down_rows[0].reshape(-1)])]
    unnamed x3 -> x9, local copies, waits for them, and re-layouts: 1.28 us -> 3 us
    convert_element_type x2 -> x0, other arithmetic: 1.59 us -> none  [the longest x1 0.82 us: per_device_fused(): keep.astype(jnp.float32)[:, None]]
    slice x2 -> x0, other arithmetic: 1.52 us -> none  [flat_rows(): return jnp.stack([index[:, 0], index[:, 1] ^ 1], axis=1).reshape(-1)]
    concatenate x2, other arithmetic: 0.04 us -> 1.02 us  [the longest x1 1.02 us: per_device_fused(): own = paired(jnp.concatenate([up_blocks[0], down_blocks[0]], axis=0))]
where the time goes in v2:
time: 64.5 us; the launch traced here: 63.5 us
  Pallas kernels  58 us (90%)
  local copies, waits for them, and re-layouts  4.4 us (7%)
  other arithmetic  1.02 us (2%)
    pallas_call x1, Pallas kernels, per_device_fused(): pl.pallas_call(functools.partial(kernel, devices // 2), out_shape=jax.Sha...  58 us
    unnamed x9, local copies, waits for them, and re-layouts  3 us

profile of v2, /device:TPU:2, one launch (start us, length us, event | category | flops | bytes accessed | tf_op | source)
XLA Modules:
  0.0 63.5 jit_solution(16088575675837852306)
XLA Ops:
  0.0 0.0 copy-start.1
  0.0 0.0 copy-start.2
  0.0 0.0 copy-start
  0.0 0.9 %copy.10 = s32[1,96,2]{2,1,0:T(8,128)S(1)} copy(s32[1,96,2]{1,2,0:T(2,128)} %param.12) | data formatting | bytes 1536 | tf_op args[5]
  0.9 0.1 reshape_squeeze.7
  1.1 0.8 %copy.9 = s32[1,192,2]{2,1,0:T(8,128)S(1)} copy(s32[1,192,2]{1,2,0:T(2,128)} %param.10) | data formatting | bytes 3072 | tf_op args[3]
  1.9 0.1 reshape_squeeze.6
  2.0 1.0 %pad_maximum_fusion = bf16[36,4096]{1,0:T(8,128)(2,1)S(1)} fusion(bf16[12,4096]{1,0:T(8,128)(2,1)} %bitcast.13, bf16[24,4096]{1,0:T(8,128)(2,1)} %bitcast.12), kind=kLoop, calls=%fused_computation | loop fusion | flops 589824 | bytes 589824 | tf_op jit(solution)/shard_map/concatenate | solution.py:381
  3.1 0.6 %reshape.10 = bf16[9,2,128,64]{3,2,1,0:T(8,128)(2,1)S(1)} reshape(bf16[36,4096]{1,0:T(8,128)(2,1)S(1)} %pad_maximum_fusion) | data formatting | bytes 589824 | tf_op jit(solution)/shard_map/reshape | solution.py:375
  3.7 0.3 copy.11
  4.0 0.2 copy.12.w_ref
  4.2 0.0 copy-done.1
  4.2 0.0 copy-done.2
  4.2 0.0 copy-done
  4.2 58.0 %shard_map.73 = bf16[160,6144]{1,0:T(8,128)(2,1)S(1)} custom-call(bf16[160,6144]{1,0:T(8,128)(2,1)S(1)} %copy-done, s32[1,160]{1,0:T(1,128)S(1)} %bitcast.9, bf16[1,6144]{1,0:T(2,128)(2,1)S(1)} %copy-done.1, s32[8,128]{1,0:T(8,128)S(1)} %pad_bitcast_fusion.rows_ref, bf16[9,128,128]{2,1,0:T(8,128)(2,1)S(1)} %copy.12.w_ref), custom_call_target="tpu_custom_call" | custom-call | tf_op jit(solution)/shard_map/pallas_call | solution.py:385
  62.2 1.3 %copy.14 = bf16[1,160,6144]{2,1,0:T(8,128)(2,1)} copy(bf16[1,160,6144]{2,1,0:T(8,128)(2,1)S(1)} %bitcast.8) | data formatting | bytes 3932160
  (2 shorter events, 0.0 us)
Async XLA Ops:
  0.0 4.2 %copy-start.1 = (bf16[1,6144]{1,0:T(2,128)(2,1)S(1)}, bf16[1,6144]{1,0:T(2,128)(2,1)}, u32[]{:S(2)}) copy-start(bf16[1,6144]{1,0:T(2,128)(2,1)} %gain_ref.1) | copy-start | bytes 36868
  0.0 4.2 %copy-start.2 = (s32[160]{0:T(256)S(1)}, s32[160]{0:T(256)}, u32[]{:S(2)}) copy-start(s32[160]{0:T(256)} %param.8) | copy-start | bytes 1924
  0.0 4.2 %copy-start = (bf16[160,6144]{1,0:T(8,128)(2,1)S(1)}, bf16[160,6144]{1,0:T(8,128)(2,1)}, u32[]{:S(2)}) copy-start(bf16[160,6144]{1,0:T(8,128)(2,1)} %x_ref.1) | copy-start | bytes 5898244
